TPU v7x, 32 devices: a whole 2x2x4 slice. The times are simulated.
32 devices in a mesh: ka: 2 (over core), slab: 16 (over z, y, x).
Axes of the slice: x: 2, y: 2, z: 4, core: 2. Of those that a mesh axis runs over, the one named last changes fastest.
Arguments:
- packet_prev: float32 [2, 128, 256, 384], P('ka', 'slab'), may hold values from -18 to 18
- packet_now: float32 [2, 128, 256, 384], P('ka', 'slab'), may hold values from -18 to 18
- potential: float32 [128, 256, 384], P('slab'), may hold values from 0.05 to 0.5
- kin_rho: float32 [128, 128], replicated, may hold values from -1 to 1, as said below
- kin_theta: float32 [256, 256], replicated, may hold values from -1 to 1, as said below
- kin_phi: float32 [384, 384], replicated, may hold values from -1 to 1, as said below
- damping: float32 [128], P('slab'), may hold values from 0.8 to 1
- inertia: float32 [128], P('slab'), may hold values from 0.05 to 0.3
- tilt: float32 [256], replicated, may hold values from 0.5 to 2
Outputs:
- packet_last: float32 [2, 128, 256, 384], P('ka', 'slab')
- packet_before: float32 [2, 128, 256, 384], P('ka', 'slab')
- intersections: float32 [2, 2], P(None, 'ka')
Inputs may be any that keep to these rules, and one draw needn't show every extreme that they name: `kin_rho`: symmetric. `kin_theta`: symmetric. `kin_phi`: symmetric.
All inputs are finite; a program needn't handle non-finite values.
Results may differ from a plain program's by a relative error of at most 0.0001.
Values sent between devices are 32-bit elements; how exact they have to be, the bound alone decides.
A program may use at most 128 MiB of HBM per device.

v0:
```python
import jax
import jax.numpy as jnp
from jax import lax
from jax.sharding import PartitionSpec as P

NR = 128
NT = 256
NP = 384
STEPS = 2
JTOT = 60
K_FIRST = 0


HI = lax.Precision.HIGHEST


def padded(cells, sides, width):
    for axis, dim in sides:
        count = lax.axis_size(axis)
        ends = count - 1
        head = lax.slice_in_dim(cells, 0, width, axis=dim)
        tail = lax.slice_in_dim(cells, cells.shape[dim] - width, cells.shape[dim], axis=dim)
        cells = jnp.concatenate(
            [
                lax.ppermute(tail, axis, [(i, (i + 1) % count) for i in range(ends)]),
                cells,
                lax.ppermute(head, axis, [((i + 1) % count, i) for i in range(ends)]),
            ],
            axis=dim,
        )
    return cells


def rho_apply(kin_rho, whole):
    return jnp.einsum("sr,rtp->stp", kin_rho, whole, precision=HI)


def apply_h(q, potential, kin_rho, kin_theta, kin_phi, inertia, tilt):
    kval = (K_FIRST + lax.axis_index("ka")).astype(jnp.float32)
    jj = float(JTOT * (JTOT + 1))
    cent = (jj - 2.0 * kval * kval) / float(JTOT * JTOT)
    lam_here = jnp.sqrt(jj - kval * (kval + 1.0)) / float(JTOT)
    lam_below = jnp.sqrt(jj - (kval - 1.0) * kval) / float(JTOT)
    near = padded(q, (("ka", 0),), 1)
    field = q[0]
    term = rho_apply(
        kin_rho, lax.all_to_all(field, "slab", split_axis=1, concat_axis=0, tiled=True)
    )
    rho_part = lax.all_to_all(term, "slab", split_axis=0, concat_axis=1, tiled=True)
    theta_part = jnp.einsum("ts,rsp->rtp", kin_theta, field, precision=HI)
    rows = field.shape[0] * field.shape[1]
    phi_part = jnp.dot(field.reshape(rows, field.shape[2]), kin_phi, precision=HI).reshape(
        field.shape
    )
    coupling = (
        inertia[:, None, None] * tilt[None, :, None] * (lam_here * near[2] + lam_below * near[0])
    )
    diag = potential + inertia[:, None, None] * cent
    total = rho_part + theta_part + phi_part + diag * field + coupling
    return total[None]


def shards(packet_prev, packet_now, potential, kin_rho, kin_theta, kin_phi, damping, inertia, tilt):
    damp = damping[None, :, None, None]
    cells = float(NR * NT * NP)
    q_prev = packet_prev
    q = packet_now
    partials = []
    for step in range(STEPS):
        image = apply_h(q, potential, kin_rho, kin_theta, kin_phi, inertia, tilt)
        q_new = damp * (2.0 * image - damp * q_prev)
        local_sum = jnp.sum(packet_now * q_new, axis=(1, 2, 3))
        partials.append(lax.psum(local_sum, "slab") / cells)
        q_prev = q
        q = q_new
    intersections = jnp.stack(partials, axis=0)
    return (q, q_prev, intersections)


def solution(mesh):
    return jax.shard_map(
        shards,
        mesh=mesh,
        in_specs=(
            P("ka", "slab", None, None),
            P("ka", "slab", None, None),
            P("slab", None, None),
            P(),
            P(),
            P(),
            P("slab"),
            P("slab"),
            P(),
        ),
        out_specs=(P("ka", "slab", None, None), P("ka", "slab", None, None), P(None, "ka")),
        check_vma=False,
    )
```

profile of v0, /device:TPU:0, one launch (start us, length us, event | category | flops | bytes accessed | tf_op | source)
XLA Modules:
  0.0 420.4 jit_solution(10612199767086044564)
XLA Ops:
  0.6 0.0 copy-start
  0.6 3.8 copy.81
  4.4 0.0 copy-start.2
  4.4 79.6 %all_to_all.72 = f32[8,256,384]{2,0,1:T(8,128)S(1)} all-to-all(f32[8,256,384]{2,0,1:T(8,128)S(1)} %copy.81), channel_id=1, replica_groups=mesh['ka'=2,'slab'=16] {'slab'}, dimensions={1} | all-to-all | bytes 6291456 | tf_op jit(solution)/shard_map/all_to_all | solution.py:47
  84.0 0.0 copy-done.2
  84.0 2.9 fusion.10
  86.9 3.5 copy.84
  90.4 4.5 %all-to-all-start.1 = ((f32[128,16,384]{2,1,0:T(8,128)}), f32[128,16,384]{2,1,0:T(8,128)}, u32[]{:S(2)}, u32[]{:S(2)}) async-start(f32[128,16,384]{2,1,0:T(8,128)} %copy.84), calls=%async_computation.1 | async-start | bytes 6291456 | tf_op jit(solution)/shard_map/all_to_all | solution.py:49
  94.9 3.5 copy.80
  98.5 1.3 collective-permute-start
  99.7 6.4 %collective-permute-start.1 = (f32[1,8,256,384]{2,3,1,0:T(8,128)}, f32[1,8,256,384]{2,3,1,0:T(8,128)}, u32[]{:S(2)}, u32[]{:S(2)}) collective-permute-start(f32[1,8,256,384]{2,3,1,0:T(8,128)} %copy.80), channel_id=1, source_target_pairs={{0,16},{1,17},{2,18},{3,19},{4,20},{5,21},{6,22},{7,23},{8,24},{9,... | collective-permute-start | bytes 9437192 | tf_op jit(solution)/shard_map/ppermute | solution.py:25
  106.2 3.5 copy.89
  109.8 0.0 copy-start.5
  109.8 0.0 copy-start.4
  109.8 0.0 copy-start.1
  109.8 3.6 copy.92
  113.3 0.0 copy-done.5
  113.3 0.0 copy-done.4
  113.4 0.1 broadcast_multiply_fusion
  113.4 0.0 copy-done.1
  113.4 8.6 %fusion.22 = f32[8,384,256]{2,1,0:T(8,128)} fusion(f32[256,256]{1,0:T(8,128)S(1)} %copy-done.1, f32[1,8,256,384]{3,2,1,0:T(8,128)} %param.10), kind=kOutput, calls=%fused_computation.29 | convolution fusion | flops 2415919104 | bytes 6553600 | tf_op jit(solution)/shard_map/ts,rsp->rtp/dot_general | solution.py:50
  122.0 33.1 %all-to-all-done.1 = f32[128,16,384]{2,1,0:T(8,128)} async-done(((f32[128,16,384]{2,1,0:T(8,128)}), f32[128,16,384]{2,1,0:T(8,128)}, u32[]{:S(2)}, u32[]{:S(2)}) %all-to-all-start.1) | async-done | bytes 3145760 | tf_op jit(solution)/shard_map/all_to_all | solution.py:49
  155.1 3.9 copy.85
  158.9 3.6 copy.86
  162.5 0.0 collective-permute-done
  162.5 0.0 collective-permute-done.1
  162.5 0.0 copy-done
  162.5 0.0 copy-done.3
  162.5 16.2 %fusion.5 = f32[1,8,256,384]{2,3,1,0:T(8,128)} fusion(f32[8,256,384]{1,2,0:T(8,128)} %copy.86, f32[8,384,256]{2,1,0:T(8,128)} %fusion.22, f32[1,8,256,384]{2,3,1,0:T(8,128)} %copy.80, f32[1,8,256,384]{2,3,1,0:T(8,128)} %copy.92, f32[1,8,256,384]{2,3,1,0:T(8,128)} %collective-permute-done.1, f32[1,8,256,384]{2,3,1,0:T(8,128)} %collective-permute-done, ...), kind=kOutput, calls=%fused_computation.9 | convolution fusion | flops 3634888704 | bytes 28909640 | tf_op jit(solution)/shard_map/dot_general | solution.py:52
  178.7 3.6 copy.93
  182.3 84.8 %all_to_all.73 = f32[8,256,384]{2,0,1:T(8,128)S(1)} all-to-all(f32[8,256,384]{2,0,1:T(8,128)} %copy.93), channel_id=1, replica_groups=mesh['ka'=2,'slab'=16] {'slab'}, dimensions={1} | all-to-all | bytes 6291456 | tf_op jit(solution)/shard_map/all_to_all | solution.py:47
  267.0 0.5 copy.95
  267.6 7.1 %fusion.15 = f32[128,16,384]{0,2,1:T(8,128)} fusion(f32[128,16,384]{2,1,0:T(8,128)S(1)} %bitcast.104, f32[128,128]{1,0:T(8,128)S(1)} %copy-done.2), kind=kOutput, calls=%fused_computation.24 | convolution fusion | flops 1207959552 | bytes 6356992 | tf_op jit(solution)/shard_map/sr,rtp->stp/dot_general | solution.py:35
  274.7 3.7 copy.97
  278.4 4.5 %all-to-all-start.3 = ((f32[128,16,384]{2,1,0:T(8,128)}), f32[128,16,384]{2,1,0:T(8,128)}, u32[]{:S(2)}, u32[]{:S(2)}) async-start(f32[128,16,384]{2,1,0:T(8,128)} %copy.97), calls=%async_computation.3 | async-start | bytes 6291456 | tf_op jit(solution)/shard_map/all_to_all | solution.py:49
  282.9 1.3 collective-permute-start.2
  284.2 6.4 %collective-permute-start.3 = (f32[1,8,256,384]{2,3,1,0:T(8,128)}, f32[1,8,256,384]{2,3,1,0:T(8,128)}, u32[]{:S(2)}, u32[]{:S(2)}) collective-permute-start(f32[1,8,256,384]{2,3,1,0:T(8,128)} %fusion.5), channel_id=1, source_target_pairs={{0,16},{1,17},{2,18},{3,19},{4,20},{5,21},{6,22},{7,23},{8,24},{9,... | collective-permute-start | bytes 9437192 | tf_op jit(solution)/shard_map/ppermute | solution.py:25
  290.6 3.5 copy.106
  294.1 6.2 %fusion.20 = f32[8,384,256]{2,1,0:T(8,128)} fusion(f32[256,256]{1,0:T(8,128)S(1)} %copy-done.1, f32[1,8,256,384]{2,3,1,0:T(8,128)} %fusion.5), kind=kOutput, calls=%fused_computation.27 | convolution fusion | flops 2415919104 | bytes 6553600 | tf_op jit(solution)/shard_map/ts,rsp->rtp/dot_general | solution.py:50
  300.3 42.7 %all-to-all-done.3 = f32[128,16,384]{2,1,0:T(8,128)} async-done(((f32[128,16,384]{2,1,0:T(8,128)}), f32[128,16,384]{2,1,0:T(8,128)}, u32[]{:S(2)}, u32[]{:S(2)}) %all-to-all-start.3) | async-done | bytes 3145760 | tf_op jit(solution)/shard_map/all_to_all | solution.py:49
  343.0 3.9 copy.98
  346.9 3.5 copy.99
  350.4 0.0 collective-permute-done.2
  350.4 0.0 collective-permute-done.3
  350.4 15.0 %multiply_reduce_fusion.1 = (f32[]{:T(128)}, f32[]{:T(128)}, f32[1,8,256,384]{2,3,1,0:T(8,128)}) fusion(f32[1,8,256,384]{2,3,1,0:T(8,128)} %copy.80, f32[1,8,256,384]{2,3,1,0:T(8,128)} %fusion.5, f32[1,8,256,384]{2,3,1,0:T(8,128)} %collective-permute-done.3, f32[]{:T(128)S(6)} %div.20, f32[1,8,256,384]{2,3,1,0:T(8,128)} %collective-permute-done.2, ...), kind=kOutput, calls=%fused_computation.23 | convolution fusion | flops 3638034432 | bytes 25763920 | tf_op jit(solution)/shard_map/dot_general | solution.py:52
  365.4 49.6 %all-reduce = (f32[1]{0:T(128)}, f32[1]{0:T(128)}) all-reduce(f32[1]{0:T(128)} %bitcast.30, f32[1]{0:T(128)} %bitcast.28), channel_id=1, replica_groups=mesh['ka'=2,'slab'=16] {'slab'}, use_global_device_ids=true, to_apply=%region_3.0 | all-reduce | flops 2 | bytes 16 | tf_op jit(solution)/shard_map/psum | solution.py:73
  416.3 3.5 copy.105
  419.9 0.6 pad_maximum_fusion
  (2 shorter events, 0.0 us)
Async XLA Ops:
  0.6 161.9 %copy-start = (f32[384,384]{1,0:T(8,128)S(1)}, f32[384,384]{1,0:T(8,128)}, u32[]{:S(2)}) copy-start(f32[384,384]{1,0:T(8,128)} %param.14) | copy-start | bytes 1769476
  4.4 79.6 %copy-start.2 = (f32[128,128]{1,0:T(8,128)S(1)}, f32[128,128]{1,0:T(8,128)}, u32[]{:S(2)}) copy-start(f32[128,128]{1,0:T(8,128)} %param.12) | copy-start | bytes 196612
  90.4 64.7 %all-to-all-start.1 = ((f32[128,16,384]{2,1,0:T(8,128)}), f32[128,16,384]{2,1,0:T(8,128)}, u32[]{:S(2)}, u32[]{:S(2)}) async-start(f32[128,16,384]{2,1,0:T(8,128)} %copy.84), calls=%async_computation.1 | async-start | bytes 6291456 | tf_op jit(solution)/shard_map/all_to_all | solution.py:49
  98.5 64.1 %collective-permute-start = (f32[1,8,256,384]{2,3,1,0:T(8,128)}, f32[1,8,256,384]{2,3,1,0:T(8,128)}, u32[]{:S(2)}, u32[]{:S(2)}) collective-permute-start(f32[1,8,256,384]{2,3,1,0:T(8,128)} %copy.80), channel_id=1, source_target_pairs={{16,0},{17,1},{18,2},{19,3},{20,4},{21,5},{22,6},{23,7},{24,8},{25... | collective-permute-start | bytes 9437192 | tf_op jit(solution)/shard_map/ppermute | solution.py:27
  99.7 62.8 %collective-permute-start.1 = (f32[1,8,256,384]{2,3,1,0:T(8,128)}, f32[1,8,256,384]{2,3,1,0:T(8,128)}, u32[]{:S(2)}, u32[]{:S(2)}) collective-permute-start(f32[1,8,256,384]{2,3,1,0:T(8,128)} %copy.80), channel_id=1, source_target_pairs={{0,16},{1,17},{2,18},{3,19},{4,20},{5,21},{6,22},{7,23},{8,24},{9,... | collective-permute-start | bytes 9437192 | tf_op jit(solution)/shard_map/ppermute | solution.py:25
  109.8 3.6 copy-start.5
  109.8 3.6 copy-start.4
  109.8 3.7 copy-start.1
  158.9 3.6 copy-start.3
  278.4 64.6 %all-to-all-start.3 = ((f32[128,16,384]{2,1,0:T(8,128)}), f32[128,16,384]{2,1,0:T(8,128)}, u32[]{:S(2)}, u32[]{:S(2)}) async-start(f32[128,16,384]{2,1,0:T(8,128)} %copy.97), calls=%async_computation.3 | async-start | bytes 6291456 | tf_op jit(solution)/shard_map/all_to_all | solution.py:49
  282.9 67.5 %collective-permute-start.2 = (f32[1,8,256,384]{2,3,1,0:T(8,128)}, f32[1,8,256,384]{2,3,1,0:T(8,128)}, u32[]{:S(2)}, u32[]{:S(2)}) collective-permute-start(f32[1,8,256,384]{2,3,1,0:T(8,128)} %fusion.5), channel_id=1, source_target_pairs={{16,0},{17,1},{18,2},{19,3},{20,4},{21,5},{22,6},{23,7},{24,8},{25... | collective-permute-start | bytes 9437192 | tf_op jit(solution)/shard_map/ppermute | solution.py:27
  284.2 66.2 %collective-permute-start.3 = (f32[1,8,256,384]{2,3,1,0:T(8,128)}, f32[1,8,256,384]{2,3,1,0:T(8,128)}, u32[]{:S(2)}, u32[]{:S(2)}) collective-permute-start(f32[1,8,256,384]{2,3,1,0:T(8,128)} %fusion.5), channel_id=1, source_target_pairs={{0,16},{1,17},{2,18},{3,19},{4,20},{5,21},{6,22},{7,23},{8,24},{9,... | collective-permute-start | bytes 9437192 | tf_op jit(solution)/shard_map/ppermute | solution.py:25
where the time goes:
time: 421 us; the launch traced here: 420 us
  blocking collectives  214 us (51%)
  waiting for transfers between devices  75.8 us (18%)
  matrix products  56 us (13%)
  local copies, waits for them, and re-layouts  47.6 us (11%)
  starting transfers between devices  24.3 us (6%)
    all_to_all x2, blocking collectives, apply_h(): lax.all_to_all(field, 'slab', split_axis=1, concat_axis=0, tiled=True)  164 us
    all_to_all x2, waiting for transfers between devices, apply_h(): lax.all_to_all(term, 'slab', split_axis=0, concat_axis=1, tiled=True)  75.8 us
    psum x1, blocking collectives, shards(): partials.append(lax.psum(local_sum, 'slab') / cells)  49.6 us
    dot_general x2, matrix products, apply_h(): jnp.dot(field.reshape(rows, field.shape[2]), kin_phi, precision=HI)  31.2 us
    unnamed x17, local copies, waits for them, and re-layouts  17.8 us
    all_to_all x4, local copies, waits for them, and re-layouts, apply_h(): lax.all_to_all(term, 'slab', split_axis=0, concat_axis=1, tiled=True)  14.8 us
    dot_general x2, matrix products, apply_h(): theta_part = jnp.einsum('ts,rsp->rtp', kin_theta, field, precision=HI)  14.8 us
    ppermute x2, starting transfers between devices, padded(): lax.ppermute(tail, axis, [(i, (i + 1) % count) for i in range(ends)])  12.8 us
  transfers between devices with their start and end apart: 6, of which 2 were waited for; matrix products, arithmetic and copies ran while one was open for 10% of the time, Pallas kernels for 0%

commit v1 on v0

--- a/solution.py
+++ b/solution.py
@@ -1,6 +1,10 @@
+import functools
+
 import jax
 import jax.numpy as jnp
 from jax import lax
+from jax.experimental import pallas as pl
+from jax.experimental.pallas import tpu as pltpu
 from jax.sharding import PartitionSpec as P
 
 NR = 128
@@ -77,9 +81,349 @@
     return (q, q_prev, intersections)
 
 
+MESH = pl.DeviceIdType.MESH
+Q0, P1, U, V = range(4)
+
+
+def split(x):
+    high = x.astype(jnp.bfloat16)
+    return high, (x - high.astype(jnp.float32)).astype(jnp.bfloat16)
+
+
+def dot3(a, b):
+    dot = functools.partial(jnp.dot, preferred_element_type=jnp.float32)
+    return dot(a[0], b[0]) + (dot(a[0], b[1]) + dot(a[1], b[0]))
+
+
+def partner(me, d, n):
+    out = 0
+    bit = 1
+    while bit < n:
+        out = out + ((me // bit + d // bit) % 2) * bit
+        bit *= 2
+    return out
+
+
+def fused(
+    n, q_in, prev_in, pot_in, rho_in, theta_in, phi_in, damp, inertia, tilt,
+    last_out, before_out, stat_out,
+    q0, prev, pot, near0, qb, p1, pb, ub, ua, vb, va, q1, near1, w, qx, ux,
+    rho_hi, rho_lo, theta_hi, theta_lo, phi_hi, phi_lo, dmine, dall, stat_mine, stat_all,
+    load_sem, out_sem, own_sem, ka_send, ka_recv, send, recv, small_send, small_recv,
+):
+    rows, nt, width = q0.shape
+    cols = qb.shape[1]
+    me = lax.axis_index("slab")
+    ka = lax.axis_index("ka")
+    peers = list(range(1, n))
+
+    loads = [
+        pltpu.make_async_copy(q_in, q0, load_sem.at[0]),
+        pltpu.make_async_copy(prev_in, prev, load_sem.at[1]),
+        pltpu.make_async_copy(pot_in, pot, load_sem.at[2]),
+    ]
+    for load in loads:
+        load.start()
+
+    barrier = pltpu.get_barrier_semaphore()
+    for d in peers:
+        pl.semaphore_signal(
+            barrier, inc=1, device_id={"slab": partner(me, d, n)}, device_id_type=MESH
+        )
+    pl.semaphore_signal(barrier, inc=1, device_id={"ka": 1 - ka}, device_id_type=MESH)
+    pl.semaphore_wait(barrier, n)
+
+    def tees(j):
+        return pl.ds(pl.multiple_of(j * cols, cols), cols)
+
+    def rhos(j):
+        return pl.ds(pl.multiple_of(j * rows, rows), rows)
+
+    def away(phase, d, src, dst):
+        there = partner(me, d, n)
+        return pltpu.make_async_remote_copy(
+            src_ref=src.at[:, tees(there), :],
+            dst_ref=dst.at[rhos(me)],
+            send_sem=send.at[phase, d],
+            recv_sem=recv.at[phase, d],
+            device_id={"slab": there},
+            device_id_type=MESH,
+        )
+
+    def away_arrival(phase, d, src, dst):
+        there = partner(me, d, n)
+        return pltpu.make_async_remote_copy(
+            src_ref=src.at[:, tees(there), :],
+            dst_ref=dst.at[rhos(there)],
+            send_sem=send.at[phase, d],
+            recv_sem=recv.at[phase, d],
+            device_id={"slab": there},
+            device_id_type=MESH,
+        )
+
+    def back(phase, d, src, dst):
+        there = partner(me, d, n)
+        return pltpu.make_async_remote_copy(
+            src_ref=src.at[rhos(there)],
+            dst_ref=dst.at[:, tees(me), :],
+            send_sem=send.at[phase, d],
+            recv_sem=recv.at[phase, d],
+            device_id={"slab": there},
+            device_id_type=MESH,
+        )
+
+    def back_arrival(phase, d, src, dst):
+        there = partner(me, d, n)
+        return pltpu.make_async_remote_copy(
+            src_ref=src.at[rhos(there)],
+            dst_ref=dst.at[:, tees(there), :],
+            send_sem=send.at[phase, d],
+            recv_sem=recv.at[phase, d],
+            device_id={"slab": there},
+            device_id_type=MESH,
+        )
+
+    def across(k, src, dst):
+        return pltpu.make_async_remote_copy(
+            src_ref=src,
+            dst_ref=dst,
+            send_sem=ka_send.at[k],
+            recv_sem=ka_recv.at[k],
+            device_id={"ka": 1 - ka},
+            device_id_type=MESH,
+        )
+
+    def small(k, d, src, dst, slot):
+        there = partner(me, d, n)
+        return pltpu.make_async_remote_copy(
+            src_ref=src,
+            dst_ref=dst.at[slot],
+            send_sem=small_send.at[k, d],
+            recv_sem=small_recv.at[k, d],
+            device_id={"slab": there},
+            device_id_type=MESH,
+        )
+
+    across(0, q_in, near0).start()
+    for d in peers:
+        away(Q0, d, q_in, qb).start()
+    own_q = pltpu.make_async_copy(q_in.at[:, tees(me), :], qb.at[rhos(me)], own_sem.at[Q0])
+    own_q.start()
+
+    for r in range(rows):
+        dmine[r : r + 1, :] = jnp.full((1, dmine.shape[1]), damp[r], jnp.float32)
+    for d in peers:
+        small(0, d, dmine, dall, me).start()
+    dall[me] = dmine[...]
+
+    for ref, high, low in (
+        (rho_in, rho_hi, rho_lo), (theta_in, theta_hi, theta_lo), (phi_in, phi_hi, phi_lo)
+    ):
+        high[...], low[...] = split(ref[...])
+
+    kval = (K_FIRST + ka).astype(jnp.float32)
+    kmin = float(K_FIRST)
+    jj = float(JTOT * (JTOT + 1))
+    cent = (jj - 2.0 * kval * kval) / float(JTOT * JTOT)
+    lam = ((jj - kmin * (kmin + 1.0)) ** 0.5) / float(JTOT)
+
+    def image(field, near, r):
+        x = field[r]
+        parts = split(x)
+        total = dot3((theta_hi[...], theta_lo[...]), parts)
+        total += dot3(parts, (phi_hi[...], phi_lo[...]))
+        total += (pot[r] + inertia[r] * cent) * x
+        slope = (inertia[r] * lam) * tilt[...]
+        return total + jnp.concatenate([slope] * (width // 128), axis=1) * near[r]
+
+    for load in loads:
+        load.wait()
+    across(0, q_in, near0).wait()
+
+    @pl.loop(0, rows)
+    def _(r):
+        p1[r] = damp[r] * (2.0 * image(q0, near0, r) - damp[r] * prev[r])
+
+    for d in peers:
+        away(Q0, d, q_in, qb).wait_send()
+        away(P1, d, p1, pb).start()
+    own_p = pltpu.make_async_copy(p1.at[:, tees(me), :], pb.at[rhos(me)], own_sem.at[P1])
+    own_p.start()
+    for d in peers:
+        away_arrival(Q0, d, q_in, qb).wait_recv()
+    own_q.wait()
+
+    chunks = [(b, c) for b in range(cols // 8) for c in range(width // 128)]
+    full = n * rows
+
+    def wide(ref, b, c):
+        return ref[:, 8 * b : 8 * b + 8, 128 * c : 128 * c + 128].reshape(full, 1024)
+
+    def narrow(ref, b, c, value):
+        ref[:, 8 * b : 8 * b + 8, 128 * c : 128 * c + 128] = value.reshape(full, 8, 128)
+
+    for i, (b, c) in enumerate(chunks):
+        x = wide(qb, b, c)
+        qx[i] = x
+        u = dot3((rho_hi[...], rho_lo[...]), split(x))
+        ux[i] = u
+        narrow(ub, b, c, u)
+
+    for d in peers:
+        away(P1, d, p1, pb).wait_send()
+        back(U, d, ub, ua).start()
+    own_u = pltpu.make_async_copy(ub.at[rhos(me)], ua.at[:, tees(me), :], own_sem.at[U])
+    own_u.start()
+    for d in peers:
+        away_arrival(P1, d, p1, pb).wait_recv()
+        small(0, d, dmine, dall, partner(me, d, n)).wait_recv()
+    own_p.wait()
+
+    dcol = 2.0 * dall[...].reshape(full, 128)
+    dwide = jnp.concatenate([dcol] * 8, axis=1)
+    acc2 = jnp.zeros((8, 128), jnp.float32)
+    for i, (b, c) in enumerate(chunks):
+        x = wide(pb, b, c) + dwide * ux[i]
+        v = dot3((rho_hi[...], rho_lo[...]), split(x))
+        narrow(vb, b, c, v)
+        prod = (qx[i] * v) * dwide
+        part = jnp.sum(prod.reshape(full // 8, 8, 1024), axis=0)
+        for k in range(8):
+            acc2 += part[:, 128 * k : 128 * k + 128]
+    stat_mine[8:16, :] = acc2
+
+    for d in peers:
+        back(U, d, ub, ua).wait_send()
+        back(V, d, vb, va).start()
+    own_v = pltpu.make_async_copy(vb.at[rhos(me)], va.at[:, tees(me), :], own_sem.at[V])
+    own_v.start()
+    for d in peers:
+        back_arrival(U, d, ub, ua).wait_recv()
+    own_u.wait()
+
+    def gather(prod):
+        part = jnp.sum(prod.reshape(nt // 8, 8, width), axis=0)
+        out = part[:, :128]
+        for k in range(1, width // 128):
+            out += part[:, 128 * k : 128 * k + 128]
+        return out
+
+    stat_mine[0:8, :] = jnp.zeros((8, 128), jnp.float32)
+
+    @pl.loop(0, rows)
+    def _(r):
+        new = p1[r] + (2.0 * damp[r]) * ua[r]
+        q1[r] = new
+        stat_mine[0:8, :] += gather(q0[r] * new)
+
+    across(1, q1, near1).start()
+    before = pltpu.make_async_copy(q1, before_out, out_sem.at[0])
+    before.start()
+    across(1, q1, near1).wait()
+
+    @pl.loop(0, rows)
+    def _(r):
+        new = damp[r] * (2.0 * image(q1, near1, r) - damp[r] * q0[r])
+        w[r] = new
+        stat_mine[8:16, :] += gather(q0[r] * new)
+
+    for d in peers:
+        small(1, d, stat_mine, stat_all, me).start()
+    stat_all[me] = stat_mine[...]
+
+    def finish(j, k):
+        for r in range(rows):
+            w[r, tees(j), :] += (2.0 * damp[r]) * va[r, tees(j), :]
+        pltpu.make_async_copy(
+            w.at[:, tees(j), :], last_out.at[:, tees(j), :], out_sem.at[1 + k]
+        ).start()
+
+    own_v.wait()
+    finish(me, 0)
+    for d in peers:
+        back_arrival(V, d, vb, va).wait_recv()
+        finish(partner(me, d, n), d)
+
+    for d in peers:
+        small(1, d, stat_mine, stat_all, partner(me, d, n)).wait_recv()
+    total = jnp.sum(stat_all[...], axis=0)
+    scale = 1.0 / float(NR * NT * NP)
+    stat_out[0:1, :] = jnp.full((1, 128), jnp.sum(total[0:8, :]) * scale, jnp.float32)
+    stat_out[1:2, :] = jnp.full((1, 128), jnp.sum(total[8:16, :]) * scale, jnp.float32)
+
+    for d in peers:
+        back(V, d, vb, va).wait_send()
+        small(0, d, dmine, dall, me).wait_send()
+        small(1, d, stat_mine, stat_all, me).wait_send()
+    before.wait()
+    for k, j in [(0, me)] + [(d, partner(me, d, n)) for d in peers]:
+        pltpu.make_async_copy(
+            w.at[:, tees(j), :], last_out.at[:, tees(j), :], out_sem.at[1 + k]
+        ).wait()
+
+
+def fused_shards(
+    packet_prev, packet_now, potential, kin_rho, kin_theta, kin_phi, damping, inertia, tilt
+):
+    n = lax.axis_size("slab")
+    _, rows, nt, width = packet_now.shape
+    cols, full = nt // n, n * rows
+    slab = pltpu.VMEM((rows, nt, width), jnp.float32)
+    turned = pltpu.VMEM((full, cols, width), jnp.float32)
+    pieces = (cols // 8) * (width // 128)
+    flat = pltpu.VMEM((pieces, full, 1024), jnp.float32)
+
+    def half(order):
+        return [pltpu.VMEM((order, order), jnp.bfloat16)] * 2
+
+    hbm = pl.BlockSpec(memory_space=pl.ANY)
+    vmem = pl.BlockSpec(memory_space=pltpu.VMEM)
+    smem = pl.BlockSpec(memory_space=pltpu.SMEM)
+    dma = pltpu.SemaphoreType.DMA
+    field = jax.ShapeDtypeStruct((rows, nt, width), jnp.float32)
+    last, before, stats = pl.pallas_call(
+        functools.partial(fused, n),
+        out_shape=(field, field, jax.ShapeDtypeStruct((2, 128), jnp.float32)),
+        in_specs=[hbm] * 3 + [vmem] * 3 + [smem] * 2 + [vmem],
+        out_specs=(hbm, hbm, vmem),
+        scratch_shapes=[
+            slab, slab, slab, slab, turned, slab, turned, turned, slab, turned, slab,
+            slab, slab, slab, flat, flat,
+            *half(full), *half(nt), *half(width),
+            pltpu.VMEM((rows, 128), jnp.float32),
+            pltpu.VMEM((n, rows, 128), jnp.float32),
+            pltpu.VMEM((16, 128), jnp.float32),
+            pltpu.VMEM((n, 16, 128), jnp.float32),
+            dma((3,)), dma((n + 1,)), dma((4,)), dma((2,)), dma((2,)),
+            dma((4, n)), dma((4, n)), dma((2, n)), dma((2, n)),
+        ],
+        compiler_params=pltpu.CompilerParams(
+            collective_id=0, has_side_effects=True, vmem_limit_bytes=60 * 2**20
+        ),
+        name="chebyshev",
+    )(
+        packet_now[0], packet_prev[0], potential, kin_rho, kin_theta, kin_phi, damping, inertia,
+        jnp.broadcast_to(tilt[:, None], (nt, 128)),
+    )
+    return last[None], before[None], stats[:, :1]
+
+
+def fits_fused(mesh):
+    n = mesh.shape["slab"]
+    return (
+        mesh.shape["ka"] == 2
+        and STEPS == 2
+        and n > 1
+        and n & (n - 1) == 0
+        and NR == 8 * n
+        and NT % (8 * n) == 0
+        and NP % 128 == 0
+    )
+
+
 def solution(mesh):
     return jax.shard_map(
-        shards,
+        fused_shards if fits_fused(mesh) else shards,
         mesh=mesh,
         in_specs=(
             P("ka", "slab", None, None),

time: 421 us -> 303 us (0.72)
  Pallas kernels: 0 us -> 294 us
  blocking collectives: 214 us -> 0 us
  waiting for transfers between devices: 75.8 us -> 0 us
  matrix products: 56 us -> 0 us
  local copies, waits for them, and re-layouts: 47.6 us -> 8.29 us
  starting transfers between devices: 24.3 us -> 0 us
    pallas_call x0 -> x1, Pallas kernels: none -> 294 us  [fused_shards(): pl.pallas_call(functools.partial(fused, n), out_shape=(field, field, jax....]
    all_to_all x2 -> x0, blocking collectives: 164 us -> none  [apply_h(): lax.all_to_all(field, 'slab', split_axis=1, concat_axis=0, tiled=True)]
    all_to_all x2 -> x0, waiting for transfers between devices: 75.8 us -> none  [apply_h(): lax.all_to_all(term, 'slab', split_axis=0, concat_axis=1, tiled=True)]
    dot_general x6 -> x0, matrix products: 56 us -> none  [the longest x2 31.2 us: apply_h(): jnp.dot(field.reshape(rows, field.shape[2]), kin_phi, precision=HI)]
    psum x1 -> x0, blocking collectives: 49.6 us -> none  [shards(): partials.append(lax.psum(local_sum, 'slab') / cells)]
    ppermute x4 -> x0, starting transfers between devices: 15.4 us -> none  [the longest x2 12.8 us: padded(): lax.ppermute(tail, axis, [(i, (i + 1) % count) for i in range(ends)])]
    all_to_all x5 -> x0, local copies, waits for them, and re-layouts: 15.3 us -> none  [the longest x4 14.8 us: apply_h(): lax.all_to_all(term, 'slab', split_axis=0, concat_axis=1, tiled=True)]
    unnamed x17 -> x5, local copies, waits for them, and re-layouts: 17.8 us -> 6.85 us
  transfers between devices with their start and end apart: 6 -> 0, of which waited for: 2 -> 0; matrix products, arithmetic and copies ran while one was open for 10% -> 0% of each run, Pallas kernels for 0% -> 0%
where the time goes in v1:
time: 303 us
  Pallas kernels  294 us (97%)
  local copies, waits for them, and re-layouts  8.29 us (3%)
    pallas_call x1, Pallas kernels, fused_shards(): pl.pallas_call(functools.partial(fused, n), out_shape=(field, field, jax....  294 us
    unnamed x5, local copies, waits for them, and re-layouts  6.85 us

profile of v1, /device:TPU:0, one launch (start us, length us, event | category | flops | bytes accessed | tf_op | source)
XLA Modules:
  0.0 303.3 jit_solution(1298632189136758490)
XLA Ops:
  0.6 1.4 broadcast_in_dim.12.tilt
  2.1 294.3 %chebyshev.1 = (f32[8,256,384]{2,1,0:T(8,128)}, f32[8,256,384]{2,1,0:T(8,128)}, f32[2,128]{1,0:T(2,128)}) custom-call(f32[8,256,384]{2,1,0:T(8,128)} %bitcast.7, f32[8,256,384]{2,1,0:T(8,128)} %bitcast.8, f32[8,256,384]{2,1,0:T(8,128)} %pot_in.1, f32[128,128]{1,0:T(8,128)} %rho_in.1, f32[256,256]{1,0:T(8,128)} %theta_in.1, f32[384,384]{1,0:T(8,128)} %phi_in.1, ...), custom_call_target="tpu_custom_call" | custom-call | tf_op jit(solution)/shard_map/chebyshev/pallas_call | solution.py:384
  296.4 1.3 copy.12
  297.7 0.0 copy-start
  297.7 3.9 %copy.15 = f32[1,8,256,384]{3,2,1,0:T(8,128)} copy(f32[1,8,256,384]{3,2,1,0:T(8,128)} %bitcast.6) | data formatting | bytes 6291456
  301.6 0.0 copy-done
  301.6 1.7 copy.16
Async XLA Ops:
  297.7 3.9 %copy-start = (f32[8,256,384]{2,1,0:T(8,128)S(1)}, f32[8,256,384]{2,1,0:T(8,128)}, u32[]{:S(2)}) copy-start(f32[8,256,384]{2,1,0:T(8,128)} %get-tuple-element.7) | copy-start | bytes 9437188

commit v2 on v1

--- a/solution.py
+++ b/solution.py
@@ -105,9 +105,10 @@
 
 
 def fused(
-    n, q_in, prev_in, pot_in, rho_in, theta_in, phi_in, damp, inertia, tilt,
+    n, q_in, prev_in, pot_in, rho_in, theta_in, phi_in, damp_in, inertia_in, tilt_in,
     last_out, before_out, stat_out,
-    q0, prev, pot, near0, qb, p1, pb, ub, ua, vb, va, q1, near1, w, qx, ux,
+    q0, prev, pot, near0, qb, p1, pb, ub, ua, vb, va, near1, qx, ux, slope,
+    rho, theta, phi, damp, inertia, tilt,
     rho_hi, rho_lo, theta_hi, theta_lo, phi_hi, phi_lo, dmine, dall, stat_mine, stat_all,
     load_sem, out_sem, own_sem, ka_send, ka_recv, send, recv, small_send, small_recv,
 ):
@@ -121,6 +122,12 @@
         pltpu.make_async_copy(q_in, q0, load_sem.at[0]),
         pltpu.make_async_copy(prev_in, prev, load_sem.at[1]),
         pltpu.make_async_copy(pot_in, pot, load_sem.at[2]),
+        pltpu.make_async_copy(rho_in, rho, load_sem.at[3]),
+        pltpu.make_async_copy(theta_in, theta, load_sem.at[4]),
+        pltpu.make_async_copy(phi_in, phi, load_sem.at[5]),
+        pltpu.make_async_copy(damp_in, damp, load_sem.at[6]),
+        pltpu.make_async_copy(inertia_in, inertia, load_sem.at[7]),
+        pltpu.make_async_copy(tilt_in, tilt, load_sem.at[8]),
     ]
     for load in loads:
         load.start()
@@ -210,14 +217,23 @@
     own_q = pltpu.make_async_copy(q_in.at[:, tees(me), :], qb.at[rhos(me)], own_sem.at[Q0])
     own_q.start()
 
+    for load in loads:
+        load.wait()
     for r in range(rows):
         dmine[r : r + 1, :] = jnp.full((1, dmine.shape[1]), damp[r], jnp.float32)
     for d in peers:
         small(0, d, dmine, dall, me).start()
     dall[me] = dmine[...]
 
+    @pl.loop(0, nt // 8)
+    def _(i):
+        at = pl.ds(pl.multiple_of(8 * i, 8), 8)
+        slope[at, :] = jnp.concatenate(
+            [jnp.full((1, 128), tilt[8 * i + k], jnp.float32) for k in range(8)], axis=0
+        )
+
     for ref, high, low in (
-        (rho_in, rho_hi, rho_lo), (theta_in, theta_hi, theta_lo), (phi_in, phi_hi, phi_lo)
+        (rho, rho_hi, rho_lo), (theta, theta_hi, theta_lo), (phi, phi_hi, phi_lo)
     ):
         high[...], low[...] = split(ref[...])
 
@@ -233,11 +249,9 @@
         total = dot3((theta_hi[...], theta_lo[...]), parts)
         total += dot3(parts, (phi_hi[...], phi_lo[...]))
         total += (pot[r] + inertia[r] * cent) * x
-        slope = (inertia[r] * lam) * tilt[...]
-        return total + jnp.concatenate([slope] * (width // 128), axis=1) * near[r]
-
-    for load in loads:
-        load.wait()
+        tilted = (inertia[r] * lam) * slope[...]
+        return total + jnp.concatenate([tilted] * (width // 128), axis=1) * near[r]
+
     across(0, q_in, near0).wait()
 
     @pl.loop(0, rows)
@@ -313,18 +327,18 @@
     @pl.loop(0, rows)
     def _(r):
         new = p1[r] + (2.0 * damp[r]) * ua[r]
-        q1[r] = new
+        p1[r] = new
         stat_mine[0:8, :] += gather(q0[r] * new)
 
-    across(1, q1, near1).start()
-    before = pltpu.make_async_copy(q1, before_out, out_sem.at[0])
+    across(1, p1, near1).start()
+    before = pltpu.make_async_copy(p1, before_out, out_sem.at[0])
     before.start()
-    across(1, q1, near1).wait()
+    across(1, p1, near1).wait()
 
     @pl.loop(0, rows)
     def _(r):
-        new = damp[r] * (2.0 * image(q1, near1, r) - damp[r] * q0[r])
-        w[r] = new
+        new = damp[r] * (2.0 * image(p1, near1, r) - damp[r] * q0[r])
+        prev[r] = new
         stat_mine[8:16, :] += gather(q0[r] * new)
 
     for d in peers:
@@ -333,9 +347,9 @@
 
     def finish(j, k):
         for r in range(rows):
-            w[r, tees(j), :] += (2.0 * damp[r]) * va[r, tees(j), :]
+            prev[r, tees(j), :] += (2.0 * damp[r]) * va[r, tees(j), :]
         pltpu.make_async_copy(
-            w.at[:, tees(j), :], last_out.at[:, tees(j), :], out_sem.at[1 + k]
+            prev.at[:, tees(j), :], last_out.at[:, tees(j), :], out_sem.at[1 + k]
         ).start()
 
     own_v.wait()
@@ -348,8 +362,8 @@
         small(1, d, stat_mine, stat_all, partner(me, d, n)).wait_recv()
     total = jnp.sum(stat_all[...], axis=0)
     scale = 1.0 / float(NR * NT * NP)
-    stat_out[0:1, :] = jnp.full((1, 128), jnp.sum(total[0:8, :]) * scale, jnp.float32)
-    stat_out[1:2, :] = jnp.full((1, 128), jnp.sum(total[8:16, :]) * scale, jnp.float32)
+    stat_out[0, 0] = jnp.sum(total[0:8, :]) * scale
+    stat_out[0, 1] = jnp.sum(total[8:16, :]) * scale
 
     for d in peers:
         back(V, d, vb, va).wait_send()
@@ -358,7 +372,7 @@
     before.wait()
     for k, j in [(0, me)] + [(d, partner(me, d, n)) for d in peers]:
         pltpu.make_async_copy(
-            w.at[:, tees(j), :], last_out.at[:, tees(j), :], out_sem.at[1 + k]
+            prev.at[:, tees(j), :], last_out.at[:, tees(j), :], out_sem.at[1 + k]
         ).wait()
 
 
@@ -376,25 +390,27 @@
     def half(order):
         return [pltpu.VMEM((order, order), jnp.bfloat16)] * 2
 
-    hbm = pl.BlockSpec(memory_space=pl.ANY)
-    vmem = pl.BlockSpec(memory_space=pltpu.VMEM)
+    hbm = pl.BlockSpec(memory_space=pltpu.HBM)
+    place = pl.BlockSpec(memory_space=pl.ANY)
     smem = pl.BlockSpec(memory_space=pltpu.SMEM)
     dma = pltpu.SemaphoreType.DMA
     field = jax.ShapeDtypeStruct((rows, nt, width), jnp.float32)
     last, before, stats = pl.pallas_call(
         functools.partial(fused, n),
-        out_shape=(field, field, jax.ShapeDtypeStruct((2, 128), jnp.float32)),
-        in_specs=[hbm] * 3 + [vmem] * 3 + [smem] * 2 + [vmem],
-        out_specs=(hbm, hbm, vmem),
+        out_shape=(field, field, jax.ShapeDtypeStruct((1, 2), jnp.float32)),
+        in_specs=[hbm] * 9,
+        out_specs=(place, place, smem),
         scratch_shapes=[
             slab, slab, slab, slab, turned, slab, turned, turned, slab, turned, slab,
-            slab, slab, slab, flat, flat,
+            slab, flat, flat, pltpu.VMEM((nt, 128), jnp.float32),
+            *[pltpu.VMEM((order, order), jnp.float32) for order in (full, nt, width)],
+            *[pltpu.SMEM((count,), jnp.float32) for count in (rows, rows, nt)],
             *half(full), *half(nt), *half(width),
             pltpu.VMEM((rows, 128), jnp.float32),
             pltpu.VMEM((n, rows, 128), jnp.float32),
             pltpu.VMEM((16, 128), jnp.float32),
             pltpu.VMEM((n, 16, 128), jnp.float32),
-            dma((3,)), dma((n + 1,)), dma((4,)), dma((2,)), dma((2,)),
+            dma((9,)), dma((n + 1,)), dma((4,)), dma((2,)), dma((2,)),
             dma((4, n)), dma((4, n)), dma((2, n)), dma((2, n)),
         ],
         compiler_params=pltpu.CompilerParams(
@@ -403,9 +419,9 @@
         name="chebyshev",
     )(
         packet_now[0], packet_prev[0], potential, kin_rho, kin_theta, kin_phi, damping, inertia,
-        jnp.broadcast_to(tilt[:, None], (nt, 128)),
-    )
-    return last[None], before[None], stats[:, :1]
+        tilt,
+    )
+    return last[None], before[None], stats.T
 
 
 def fits_fused(mesh):

time: 303 us -> 300 us (0.990)
    unnamed x5 -> x7, local copies, waits for them, and re-layouts: 6.85 us -> 6.11 us
where the time goes in v2:
time: 300 us
  Pallas kernels  293 us (98%)
  local copies, waits for them, and re-layouts  6.11 us (2%)
    pallas_call x1, Pallas kernels, fused_shards(): pl.pallas_call(functools.partial(fused, n), out_shape=(field, field, jax....  293 us
    unnamed x7, local copies, waits for them, and re-layouts  6.11 us

profile of v2, /device:TPU:0, one launch (start us, length us, event | category | flops | bytes accessed | tf_op | source)
XLA Modules:
  0.0 299.9 jit_solution(7922648032016498656)
XLA Ops:
  0.6 293.2 %chebyshev.1 = (f32[8,256,384]{2,1,0:T(8,128)}, f32[8,256,384]{2,1,0:T(8,128)}, f32[1,2]{1,0:T(1,128)}) custom-call(f32[8,256,384]{2,1,0:T(8,128)} %bitcast.7, f32[8,256,384]{2,1,0:T(8,128)} %bitcast.8, f32[8,256,384]{2,1,0:T(8,128)} %pot_in.1, f32[128,128]{1,0:T(8,128)} %rho_in.1, f32[256,256]{1,0:T(8,128)} %theta_in.1, f32[384,384]{1,0:T(8,128)} %phi_in.1, ...), custom_call_target="tpu_custom_call" | custom-call | tf_op jit(solution)/shard_map/chebyshev/pallas_call | solution.py:398
  293.8 0.0 copy-start
  293.8 3.9 %copy.15 = f32[1,8,256,384]{3,2,1,0:T(8,128)} copy(f32[1,8,256,384]{3,2,1,0:T(8,128)} %bitcast.6) | data formatting | bytes 6291456
  297.7 0.0 copy-done
  297.8 0.0 copy-start.1
  297.8 1.7 copy.16
  299.4 0.0 copy-done.1
  299.4 0.5 copy.17
Async XLA Ops:
  293.8 3.9 %copy-start = (f32[8,256,384]{2,1,0:T(8,128)S(1)}, f32[8,256,384]{2,1,0:T(8,128)}, u32[]{:S(2)}) copy-start(f32[8,256,384]{2,1,0:T(8,128)} %get-tuple-element.7) | copy-start | bytes 9437188
  297.8 1.7 copy-start.1

commit v3 on v2

--- a/solution.py
+++ b/solution.py
@@ -116,7 +116,10 @@
     cols = qb.shape[1]
     me = lax.axis_index("slab")
     ka = lax.axis_index("ka")
-    peers = list(range(1, n))
+    half = n // 2
+    peers = [half]
+    for d in range(1, half):
+        peers += [d, half + d]
 
     loads = [
         pltpu.make_async_copy(q_in, q0, load_sem.at[0]),

time: 300 us -> 300 us (level)
  no operation moved by 1% of the time
where the time goes in v3:
time: 300 us
  Pallas kernels  293 us (98%)
  local copies, waits for them, and re-layouts  6.11 us (2%)
    pallas_call x1, Pallas kernels, fused_shards(): pl.pallas_call(functools.partial(fused, n), out_shape=(field, field, jax....  293 us
    unnamed x7, local copies, waits for them, and re-layouts  6.11 us

profile of v3, /device:TPU:0, one launch (start us, length us, event | category | flops | bytes accessed | tf_op | source)
XLA Modules:
  0.0 300.2 jit_solution(10637039110465263706)
XLA Ops:
  0.6 293.4 %chebyshev.1 = (f32[8,256,384]{2,1,0:T(8,128)}, f32[8,256,384]{2,1,0:T(8,128)}, f32[1,2]{1,0:T(1,128)}) custom-call(f32[8,256,384]{2,1,0:T(8,128)} %bitcast.7, f32[8,256,384]{2,1,0:T(8,128)} %bitcast.8, f32[8,256,384]{2,1,0:T(8,128)} %pot_in.1, f32[128,128]{1,0:T(8,128)} %rho_in.1, f32[256,256]{1,0:T(8,128)} %theta_in.1, f32[384,384]{1,0:T(8,128)} %phi_in.1, ...), custom_call_target="tpu_custom_call" | custom-call | tf_op jit(solution)/shard_map/chebyshev/pallas_call | solution.py:401
  294.0 0.0 copy-start
  294.0 3.9 %copy.15 = f32[1,8,256,384]{3,2,1,0:T(8,128)} copy(f32[1,8,256,384]{3,2,1,0:T(8,128)} %bitcast.6) | data formatting | bytes 6291456
  298.0 0.0 copy-done
  298.0 0.0 copy-start.1
  298.0 1.7 copy.16
  299.6 0.0 copy-done.1
  299.6 0.5 copy.17
Async XLA Ops:
  294.0 3.9 %copy-start = (f32[8,256,384]{2,1,0:T(8,128)S(1)}, f32[8,256,384]{2,1,0:T(8,128)}, u32[]{:S(2)}) copy-start(f32[8,256,384]{2,1,0:T(8,128)} %get-tuple-element.7) | copy-start | bytes 9437188
  298.0 1.7 copy-start.1
